TPU v7x, 256 devices: a whole 4x4x8 slice. The times are simulated.
256 devices in a mesh: fsdp: 64 (over x, z, y_lo), tile: 4 (over y_hi, core).
Axes of the slice: x: 4, y: 4 (y_hi: 2, y_lo: 2; y = y_hi * 2 + y_lo), z: 8, core: 2. Of those that a mesh axis runs over, the one named last changes fastest.
Arguments:
- tokens: bfloat16 [65536, 1536], P('fsdp', 'tile'), may hold values from -6 to 6
- ln_gain: float32 [1536], replicated, may hold values from 0.25 to 1.75
- w_up: bfloat16 [1536, 6144], P('fsdp', 'tile'), may hold values from -0.15625 to 0.15625
- w_down: bfloat16 [6144, 1536], P('tile', 'fsdp'), may hold values from -0.078125 to 0.078125
- w_flux_in: bfloat16 [1536, 768], P('tile'), may hold values from -0.15625 to 0.15625
- w_flux_out: bfloat16 [768, 128], replicated, may hold values from -0.21875 to 0.21875
- ocean_state: bfloat16 [2048, 128, 256], P('fsdp', 'tile'), may hold values from -6 to 6
- land_mask: int32 [2048, 128], P('fsdp', 'tile'), may hold values from 0 to 1, as said below
- column_map: int32 [2048, 128], P('fsdp', 'tile'), may hold values from 0 to 65535, as said below
- w_couple: bfloat16 [128, 256], replicated, may hold values from -0.5 to 0.5
- dw_kernel: float32 [2, 7, 7, 256], replicated, may hold values from -0.875 to 0.875
- ocean_gain: float32 [2, 256], replicated, may hold values from 0.25 to 1.75
- w_pw1: bfloat16 [2, 256, 1024], replicated, may hold values from -0.375 to 0.375
- w_pw2: bfloat16 [2, 1024, 256], replicated, may hold values from -0.1875 to 0.1875
Outputs:
- atm_out: bfloat16 [65536, 1536], P('fsdp', 'tile')
- ocean_out: bfloat16 [2048, 128, 256], P('fsdp', 'tile')
Inputs may be any that keep to these rules, and one draw needn't show every extreme that they name: `land_mask`: 0 or 1; land comes in regions of 8 x 8 cells whose ocean share varies. `column_map`: the column in grid row x names a token between (x // 32) * 1024 - 256 and (x // 32 + 1) * 1024 + 255.
All inputs are finite; a program needn't handle non-finite values.
Results may differ from a plain program's by a relative error of at most 0.014.
Values may be sent and summed in bfloat16 or wider, within the bound.
A program may use at most 128 MiB of HBM per device.

v0:
```python
import jax
import jax.numpy as jnp
from jax import lax
from jax.sharding import PartitionSpec as P


def with_halo(block, sides, width):
    for axis, dim in sides:
        count = lax.axis_size(axis)
        forward = [(i, i + 1) for i in range(count - 1)]
        backward = [(target, source) for source, target in forward]
        low = lax.ppermute(
            lax.slice_in_dim(block, block.shape[dim] - width, None, axis=dim), axis, forward
        )
        high = lax.ppermute(lax.slice_in_dim(block, 0, width, axis=dim), axis, backward)
        block = jnp.concatenate([low, block, high], axis=dim)
    return block


def layer_norm(values, gain):
    center = values - jnp.mean(values, axis=-1, keepdims=True)
    spread = jnp.mean(center * center, axis=-1, keepdims=True)
    return center * lax.rsqrt(spread + 1e-06) * gain


def conv_block(padded, region_mask, kernel, gain, w_one, w_two):
    rows = padded.shape[0] - 6
    cols = padded.shape[1] - 6
    chans = padded.shape[2]
    total = jnp.zeros((rows, cols, chans), jnp.float32)
    for first in range(7):
        for second in range(7):
            total = (
                total
                + padded[first : first + rows, second : second + cols].astype(jnp.float32)
                * kernel[first, second]
            )
    pnorm = layer_norm(total, gain).astype(jnp.bfloat16).reshape(rows * cols, chans)
    inner = jax.nn.gelu(
        jnp.dot(pnorm, w_one, preferred_element_type=jnp.float32), approximate=True
    ).astype(jnp.bfloat16)
    lowered = jnp.dot(inner, w_two, preferred_element_type=jnp.float32).reshape(rows, cols, chans)
    before = padded[3 : 3 + rows, 3 : 3 + cols].astype(jnp.float32)
    return (region_mask[..., None] * (before + lowered)).astype(jnp.bfloat16)


def body(
    tokens,
    ln_gain,
    w_up,
    w_down,
    w_flux_in,
    w_flux_out,
    ocean_state,
    land_mask,
    column_map,
    w_couple,
    dw_kernel,
    ocean_gain,
    w_pw1,
    w_pw2,
):
    band_rows = tokens.shape[0]
    whole = lax.all_gather(tokens, "tile", axis=1, tiled=True)
    normed = layer_norm(whole.astype(jnp.float32), ln_gain).astype(jnp.bfloat16)
    up_whole = lax.all_gather(w_up, "fsdp", axis=0, tiled=True)
    pre = jnp.dot(normed, up_whole, preferred_element_type=jnp.float32)
    hidden = jax.nn.gelu(pre, approximate=True).astype(jnp.bfloat16)
    down_whole = lax.all_gather(w_down, "fsdp", axis=1, tiled=True)
    terms = jnp.dot(hidden, down_whole, preferred_element_type=jnp.float32)
    delta = lax.psum_scatter(terms, "tile", scatter_dimension=1, tiled=True)
    atm_out = (tokens.astype(jnp.float32) + delta).astype(jnp.bfloat16)
    flux_pre = lax.psum(jnp.dot(atm_out, w_flux_in, preferred_element_type=jnp.float32), "tile")
    flux_hidden = jax.nn.gelu(flux_pre, approximate=True).astype(jnp.bfloat16)
    fluxes = jnp.dot(flux_hidden, w_flux_out, preferred_element_type=jnp.float32).astype(
        jnp.bfloat16
    )
    rim_rows = band_rows // 4
    window = with_halo(fluxes, (("fsdp", 0),), rim_rows)
    band = lax.axis_index("fsdp")
    local_index = (column_map - (band * band_rows - rim_rows)).reshape(-1)
    picked = jnp.take(window, local_index, axis=0)
    grid_rows = ocean_state.shape[0]
    grid_cols = ocean_state.shape[1]
    chans = ocean_state.shape[2]
    forcing = jnp.dot(picked, w_couple, preferred_element_type=jnp.float32).reshape(
        grid_rows, grid_cols, chans
    )
    mask = land_mask.astype(jnp.float32)
    state = (mask[..., None] * (ocean_state.astype(jnp.float32) + forcing)).astype(jnp.bfloat16)
    count = dw_kernel.shape[0]
    for block in range(count):
        padded = with_halo(state, (("fsdp", 0), ("tile", 1)), 3)
        state = conv_block(
            padded, mask, dw_kernel[block], ocean_gain[block], w_pw1[block], w_pw2[block]
        )
    return (atm_out, state)


def solution(mesh):
    placed = (
        P("fsdp", "tile"),
        P(),
        P("fsdp", "tile"),
        P("tile", "fsdp"),
        P("tile", None),
        P(),
        P("fsdp", "tile", None),
        P("fsdp", "tile"),
        P("fsdp", "tile"),
        P(),
        P(),
        P(),
        P(),
        P(),
    )
    return jax.shard_map(
        body,
        mesh=mesh,
        in_specs=placed,
        out_specs=(P("fsdp", "tile"), P("fsdp", "tile", None)),
        check_vma=False,
    )
```

profile of v0, /device:TPU:7, one launch (start us, length us, event | category | flops | bytes accessed | tf_op | source)
XLA Modules:
  0.0 921.2 jit_solution(5960225791835715964)
XLA Ops:
  9.5 38.8 %all-gather.4.cloned.1.call-done = bf16[1024,1536]{1,0:T(8,128)(2,1)} async-done(((bf16[1024,384]{1,0:T(8,128)(2,1)}), bf16[1024,1536]{1,0:T(8,128)(2,1)}) %all-gather.4.cloned.1.call-update) | async-done | bytes 3145744 | tf_op jit(solution)/shard_map/all_gather | solution.py:64
  48.3 2.5 convert_reduce_fusion
  51.1 1.0 fusion.2
  52.1 237.8 %all-gather.6.cloned.1.call-done = bf16[1536,1536]{1,0:T(8,128)(2,1)} async-done(((bf16[24,1536]{1,0:T(8,128)(2,1)}), bf16[1536,1536]{1,0:T(8,128)(2,1)}) %all-gather.6.cloned.1.call-update) | async-done | bytes 4718608 | tf_op jit(solution)/shard_map/all_gather | solution.py:66
  289.9 304.7 %all-gather.8.cloned.1.call-done = bf16[1536,1536]{0,1:T(8,128)(2,1)} async-done(((bf16[1536,24]{0,1:T(8,128)(2,1)}), bf16[1536,1536]{0,1:T(8,128)(2,1)}) %all-gather.8.cloned.1.call-update) | async-done | bytes 4718608 | tf_op jit(solution)/shard_map/all_gather | solution.py:69
  594.6 17.4 %fusion.37 = f32[1024,1536]{1,0:T(8,128)} fusion(bf16[1536,1536]{0,1:T(8,128)(2,1)} %all-gather.8.cloned.1.call-done, bf16[1536,1536]{1,0:T(8,128)(2,1)} %all-gather.6.cloned.1.call-done, bf16[1024,1536]{1,0:T(8,128)(2,1)} %all-gather.4.cloned.1.call-done, f32[1536]{0:T(1024)S(1)} %copy-done.13, f32[1024]{0:T(1024)S(1)} %add_rsqrt_fusion.2, ...), kind=kOutput, calls=%fused_computation.44 | convolution fusion | flops 9685696512 | bytes 18888704 | tf_op jit(solution)/shard_map/dot_general | solution.py:70
  612.0 132.7 %reduce-scatter.2.cloned.1.call-done = f32[1024,384]{1,0:T(8,128)} async-done(((f32[1024,1536]{1,0:T(8,128)}), f32[1024,384]{1,0:T(8,128)}) %reduce-scatter.2.cloned.1.call-update) | async-done | bytes 1572880 | tf_op jit(solution)/shard_map/reduce_scatter | solution.py:71
  744.7 1.6 add_convert_fusion
  746.4 2.7 fusion.155
  749.5 80.5 %all-reduce.2.cloned.1.call-done = f32[1024,768]{1,0:T(8,128)} async-done(((f32[1024,768]{1,0:T(8,128)}), f32[1024,768]{1,0:T(8,128)}) %all-reduce.2.cloned.1.call-update) | async-done | bytes 3145744 | tf_op jit(solution)/shard_map/psum | solution.py:73
  830.0 3.0 fusion.58
  833.1 2.3 collective-permute-start
  835.5 6.3 collective-permute-start.1
  841.8 1.6 collective-permute-done.1
  843.4 3.2 gather_fusion
  847.3 2.0 collective-permute-start.2
  849.3 6.2 collective-permute-start.3
  855.6 1.1 collective-permute-done.3
  856.8 4.5 collective-permute-start.4
  861.4 1.9 collective-permute-start.5
  863.3 5.3 collective-permute-done.5
  869.1 9.1 fusion.142
  879.0 1.5 fusion.20
  881.2 1.9 collective-permute-start.6
  883.1 6.4 collective-permute-start.7
  889.6 1.1 collective-permute-done.7
  890.8 3.3 collective-permute-start.8
  894.1 2.1 collective-permute-start.9
  896.2 5.0 collective-permute-done.9
  901.8 9.1 fusion.140
  911.7 1.5 fusion.28
  913.1 1.5 fusion.57
  (80 shorter events, 7.0 us)
Async XLA Ops:
  7.2 739.2 %copy-start = (bf16[384,768]{1,0:T(8,128)(2,1)S(1)}, bf16[384,768]{1,0:T(8,128)(2,1)}, u32[]{:S(2)}) copy-start(bf16[384,768]{1,0:T(8,128)(2,1)} %param.18) | copy-start | bytes 1769476
  7.2 41.1 %all-gather.4.cloned.1.call-start = ((), (), s32[]{:S(2)}) async-start(), calls=%async_computation.1 | async-start | bytes 3932160 | tf_op jit(solution)/shard_map/all_gather | solution.py:64
  7.9 281.9 %all-gather.6.cloned.1.call-start = ((), (), s32[]{:S(2)}) async-start(), calls=%async_computation.2 | async-start | bytes 4792320 | tf_op jit(solution)/shard_map/all_gather | solution.py:66
  8.7 585.9 %all-gather.8.cloned.1.call-start = ((), (), s32[]{:S(2)}) async-start(), calls=%async_computation.3 | async-start | bytes 4792320 | tf_op jit(solution)/shard_map/all_gather | solution.py:69
  9.4 585.2 %copy-start.13 = (f32[1536]{0:T(1024)S(1)}, f32[1536]{0:T(1024)}, u32[]{:S(2)}) copy-start(f32[1536]{0:T(1024)} %param.15) | copy-start | bytes 18436
  9.4 735.3 %reduce-scatter.2.cloned.1.call-start = ((), (), s32[]{:S(2)}) async-start(), calls=%async_computation.4 | async-start | bytes 7864320 | tf_op jit(solution)/shard_map/reduce_scatter | solution.py:71
  48.3 2.8 copy-start.1
  612.0 132.7 %copy-start.2 = (bf16[1024,384]{1,0:T(8,128)(2,1)S(1)}, bf16[1024,384]{1,0:T(8,128)(2,1)}, u32[]{:S(2)}) copy-start(bf16[1024,384]{1,0:T(8,128)(2,1)} %param.14) | copy-start | bytes 2359300
  612.0 218.1 %all-reduce.2.cloned.1.call-start = ((), (), s32[]{:S(2)}) async-start(), calls=%async_computation.5 | async-start | bytes 6291456 | tf_op jit(solution)/shard_map/psum | solution.py:73
  746.3 2.8 copy-start.3
  746.3 2.8 copy-start.7
  746.3 2.9 copy-start.5
  746.4 83.7 %copy-start.12 = (bf16[768,128]{1,0:T(8,128)(2,1)S(1)}, bf16[768,128]{1,0:T(8,128)(2,1)}, u32[]{:S(2)}) copy-start(bf16[768,128]{1,0:T(8,128)(2,1)} %param.19) | copy-start | bytes 589828
  749.5 92.3 %copy-start.8 = (s32[32,32]{1,0:T(8,128)S(1)}, s32[32,32]{1,0:T(8,128)}, u32[]{:S(2)}) copy-start(s32[32,32]{1,0:T(8,128)} %param.21) | copy-start | bytes 12292
  833.1 13.6 %copy-start.6 = (bf16[128,256]{1,0:T(8,128)(2,1)S(1)}, bf16[128,256]{1,0:T(8,128)(2,1)}, u32[]{:S(2)}) copy-start(bf16[128,256]{1,0:T(8,128)(2,1)} %param.23) | copy-start | bytes 196612
  833.1 13.9 %copy-start.4 = (bf16[32,32,256]{2,1,0:T(8,128)(2,1)S(1)}, bf16[32,32,256]{2,1,0:T(8,128)(2,1)}, u32[]{:S(2)}) copy-start(bf16[32,32,256]{2,1,0:T(8,128)(2,1)} %param.20) | copy-start | bytes 1572868
  833.1 8.7 collective-permute-start
  835.5 7.9 collective-permute-start.1
  843.4 19.9 %copy-start.9 = (f32[2,256]{1,0:T(2,128)S(1)}, f32[2,256]{1,0:T(2,128)}, u32[]{:S(2)}) copy-start(f32[2,256]{1,0:T(2,128)} %param.25) | copy-start | bytes 6148
  847.3 8.3 collective-permute-start.2
  849.3 7.4 collective-permute-start.3
  856.8 6.5 collective-permute-start.4
  861.4 7.2 collective-permute-start.5
  869.1 9.9 %copy-start.10 = (bf16[2,256,1024]{2,1,0:T(8,128)(2,1)S(1)}, bf16[2,256,1024]{2,1,0:T(8,128)(2,1)}, u32[]{:S(2)}) copy-start(bf16[2,256,1024]{2,1,0:T(8,128)(2,1)} %param.26) | copy-start | bytes 3145732
  879.0 1.5 copy-start.11
  881.2 8.3 collective-permute-start.6
  883.1 7.5 collective-permute-start.7
  890.8 5.5 collective-permute-start.8
  894.1 7.2 collective-permute-start.9
Sparse Core Ops, SparseCore 0:
  9.8 38.4 all-gather.3
  50.1 239.7 all-gather.5
  291.7 302.8 all-gather.7
  612.1 132.5 reduce-scatter.1
  749.2 80.8 all-reduce.1
where the time goes:
time: 922 us; the launch traced here: 921 us
  waiting for transfers between devices  811 us (88%)
  starting transfers between devices  37.3 us (4%)
  matrix products  28.7 us (3%)
  other arithmetic  26.2 us (3%)
  between operations  14.3 us (2%)
    all_gather x1, waiting for transfers between devices, body(): down_whole = lax.all_gather(w_down, 'fsdp', axis=1, tiled=True)  305 us
    all_gather x1, waiting for transfers between devices, body(): up_whole = lax.all_gather(w_up, 'fsdp', axis=0, tiled=True)  238 us
    reduce_scatter x1, waiting for transfers between devices, body(): delta = lax.psum_scatter(terms, 'tile', scatter_dimension=1, tiled=True)  133 us
    psum x1, waiting for transfers between devices, body(): lax.psum(jnp.dot(atm_out, w_flux_in, preferred_element_type=jnp.float32),...  80.5 us
    all_gather x1, waiting for transfers between devices, body(): whole = lax.all_gather(tokens, 'tile', axis=1, tiled=True)  38.8 us
    ppermute x5, starting transfers between devices, with_halo(): lax.ppermute(lax.slice_in_dim(block, 0, width, axis=dim), axis, backward)  22.9 us
    reduce_sum x3, other arithmetic, layer_norm(): center = values - jnp.mean(values, axis=-1, keepdims=True)  20.7 us
  transfers between devices with their start and end apart: 15, of which 10 were waited for; matrix products, arithmetic and copies ran while one was open for 0% of the time, Pallas kernels for 0%

commit v1 on v0

--- a/solution.py
+++ b/solution.py
@@ -61,7 +61,8 @@
     w_pw2,
 ):
     band_rows = tokens.shape[0]
-    whole = lax.all_gather(tokens, "tile", axis=1, tiled=True)
+    stack = jnp.stack([tokens] * lax.axis_size("tile"))
+    whole = jnp.concatenate(lax.all_to_all(stack, "tile", 0, 0), axis=1)
     normed = layer_norm(whole.astype(jnp.float32), ln_gain).astype(jnp.bfloat16)
     up_whole = lax.all_gather(w_up, "fsdp", axis=0, tiled=True)
     pre = jnp.dot(normed, up_whole, preferred_element_type=jnp.float32)

time: 922 us -> 887 us (0.962)
  waiting for transfers between devices: 811 us -> 713 us
  blocking collectives: 0 us -> 60.5 us
    all_to_all x0 -> x1, blocking collectives: none -> 60.5 us  [body(): whole = jnp.concatenate(lax.all_to_all(stack, 'tile', 0, 0), axis=1)]
    all_gather x1, waiting for transfers between devices: 238 us -> 180 us  [body(): up_whole = lax.all_gather(w_up, 'fsdp', axis=0, tiled=True)]
    all_gather x1 -> x0, waiting for transfers between devices: 38.8 us -> none  [body(): whole = lax.all_gather(tokens, 'tile', axis=1, tiled=True)]
  transfers between devices with their start and end apart: 15 -> 14, of which waited for: 10 -> 9; matrix products, arithmetic and copies ran while one was open for 0% -> 1% of each run, Pallas kernels for 0% -> 0%
where the time goes in v1:
time: 887 us
  waiting for transfers between devices  713 us (80%)
  blocking collectives  60.5 us (7%)
  starting transfers between devices  37.2 us (4%)
  matrix products  29.6 us (3%)
  other arithmetic  26.8 us (3%)
  between operations  14.3 us (2%)
    all_gather x1, waiting for transfers between devices, body(): down_whole = lax.all_gather(w_down, 'fsdp', axis=1, tiled=True)  304 us
    all_gather x1, waiting for transfers between devices, body(): up_whole = lax.all_gather(w_up, 'fsdp', axis=0, tiled=True)  180 us
    reduce_scatter x1, waiting for transfers between devices, body(): delta = lax.psum_scatter(terms, 'tile', scatter_dimension=1, tiled=True)  132 us
    psum x1, waiting for transfers between devices, body(): lax.psum(jnp.dot(atm_out, w_flux_in, preferred_element_type=jnp.float32),...  80.6 us
    all_to_all x1, blocking collectives, body(): whole = jnp.concatenate(lax.all_to_all(stack, 'tile', 0, 0), axis=1)  60.5 us
    ppermute x5, starting transfers between devices, with_halo(): lax.ppermute(lax.slice_in_dim(block, 0, width, axis=dim), axis, backward)  22.8 us
    reduce_sum x3, other arithmetic, layer_norm(): center = values - jnp.mean(values, axis=-1, keepdims=True)  18.8 us
    dot_general x1, matrix products, body(): terms = jnp.dot(hidden, down_whole, preferred_element_type=jnp.float32)  18.4 us
  transfers between devices with their start and end apart: 14, of which 9 were waited for; matrix products, arithmetic and copies ran while one was open for 1% of the time, Pallas kernels for 0%

profile of v1, /device:TPU:7, one launch (start us, length us, event | category | flops | bytes accessed | tf_op | source)
XLA Modules:
  0.0 886.6 jit_solution(5995068278365710750)
XLA Ops:
  8.7 1.4 copy.16
  10.5 60.5 %all_to_all.5 = bf16[4,1024,384]{1,2,0:T(8,128)(2,1)S(1)} all-to-all(bf16[4,1024,384]{1,2,0:T(8,128)(2,1)S(1)} %stack.2), channel_id=1, replica_groups=mesh['fsdp'=64,'tile'=4] {'tile'}, dimensions={0} | all-to-all | bytes 6291456 | tf_op jit(solution)/shard_map/all_to_all | solution.py:65
  72.6 2.6 fusion.10
  75.1 180.2 %all-gather.3.cloned.1.call-done = bf16[1536,1536]{1,0:T(8,128)(2,1)} async-done(((bf16[24,1536]{1,0:T(8,128)(2,1)}), bf16[1536,1536]{1,0:T(8,128)(2,1)}) %all-gather.3.cloned.1.call-update) | async-done | bytes 4718608 | tf_op jit(solution)/shard_map/all_gather | solution.py:67
  255.3 303.7 %all-gather.5.cloned.1.call-done = bf16[1536,1536]{0,1:T(8,128)(2,1)} async-done(((bf16[1536,24]{0,1:T(8,128)(2,1)}), bf16[1536,1536]{0,1:T(8,128)(2,1)}) %all-gather.5.cloned.1.call-update) | async-done | bytes 4718608 | tf_op jit(solution)/shard_map/all_gather | solution.py:70
  559.0 18.4 %fusion.35 = f32[1024,1536]{1,0:T(8,128)} fusion(bf16[1536,1536]{0,1:T(8,128)(2,1)} %all-gather.5.cloned.1.call-done, bf16[1024,1536]{0,1:T(8,128)(2,1)} %fusion.10, bf16[1536,1536]{1,0:T(8,128)(2,1)} %all-gather.3.cloned.1.call-done), kind=kOutput, calls=%fused_computation.42 | convolution fusion | flops 9677832192 | bytes 18874368 | tf_op jit(solution)/shard_map/dot_general | solution.py:71
  577.6 132.5 %reduce-scatter.2.cloned.1.call-done = f32[1024,384]{1,0:T(8,128)} async-done(((f32[1024,1536]{1,0:T(8,128)}), f32[1024,384]{1,0:T(8,128)}) %reduce-scatter.2.cloned.1.call-update) | async-done | bytes 1572880 | tf_op jit(solution)/shard_map/reduce_scatter | solution.py:72
  710.1 1.6 add_convert_fusion
  711.8 2.7 fusion.146
  714.9 80.6 %all-reduce.2.cloned.1.call-done = f32[1024,768]{1,0:T(8,128)} async-done(((f32[1024,768]{1,0:T(8,128)}), f32[1024,768]{1,0:T(8,128)}) %all-reduce.2.cloned.1.call-update) | async-done | bytes 3145744 | tf_op jit(solution)/shard_map/psum | solution.py:74
  795.5 3.0 fusion.47
  798.5 2.3 collective-permute-start
  800.9 6.1 collective-permute-start.1
  807.0 1.8 collective-permute-done.1
  808.9 3.2 gather_fusion
  812.7 2.0 collective-permute-start.2
  814.8 6.2 collective-permute-start.3
  821.1 1.1 collective-permute-done.3
  822.3 4.5 collective-permute-start.4
  826.8 1.9 collective-permute-start.5
  828.7 5.3 collective-permute-done.5
  834.5 9.1 %fusion.131 = (f32[32,32]{1,0:T(8,128)S(1)}, f32[32,32,256]{2,1,0:T(8,128)S(1)}) fusion(f32[256]{0:T(256)S(1)} %bitcast.188, bf16[38,35,256]{2,1,0:T(8,128)(2,1)S(1)} %get-tuple-element.11, f32[256]{0:T(256)S(1)} %bitcast.189, f32[256]{0:T(256)S(1)} %bitcast.190, f32[256]{0:T(256)S(1)} %bitcast.191, bf16[3,32,256]{2,1,0:T(8,128)(2,1)S(1)} %collective-permute-done.3, ...), kind=kLoop, calls=%fused_computation.188 | loop fusion | flops 40107008 | bytes 23745536 | tf_op jit(solution)/shard_map/reduce_sum | solution.py:21
  844.4 1.5 fusion.18
  846.7 1.9 collective-permute-start.6
  848.6 6.4 collective-permute-start.7
  855.0 1.1 collective-permute-done.7
  856.2 3.3 collective-permute-start.8
  859.5 2.1 collective-permute-start.9
  861.7 5.0 collective-permute-done.9
  867.2 9.1 %fusion.129 = (f32[32,32]{1,0:T(8,128)S(1)}, f32[32,32,256]{2,1,0:T(8,128)S(1)}) fusion(f32[256]{0:T(256)S(1)} %bitcast.150, bf16[38,35,256]{2,1,0:T(8,128)(2,1)S(1)} %get-tuple-element.7, f32[256]{0:T(256)S(1)} %bitcast.151, f32[256]{0:T(256)S(1)} %bitcast.152, f32[256]{0:T(256)S(1)} %bitcast.153, bf16[3,32,256]{2,1,0:T(8,128)(2,1)S(1)} %collective-permute-done.7, ...), kind=kLoop, calls=%fused_computation.187 | loop fusion | flops 40107008 | bytes 23745536 | tf_op jit(solution)/shard_map/reduce_sum | solution.py:21
  877.1 1.5 fusion.26
  878.6 1.5 fusion.46
  (79 shorter events, 8.1 us)
Async XLA Ops:
  7.2 704.6 %copy-start = (bf16[384,768]{1,0:T(8,128)(2,1)S(1)}, bf16[384,768]{1,0:T(8,128)(2,1)}, u32[]{:S(2)}) copy-start(bf16[384,768]{1,0:T(8,128)(2,1)} %param.18) | copy-start | bytes 1769476
  7.2 248.1 %all-gather.3.cloned.1.call-start = ((), (), s32[]{:S(2)}) async-start(), calls=%async_computation.2 | async-start | bytes 4792320 | tf_op jit(solution)/shard_map/all_gather | solution.py:67
  7.9 551.1 %all-gather.5.cloned.1.call-start = ((), (), s32[]{:S(2)}) async-start(), calls=%async_computation.3 | async-start | bytes 4792320 | tf_op jit(solution)/shard_map/all_gather | solution.py:70
  8.7 701.5 %reduce-scatter.2.cloned.1.call-start = ((), (), s32[]{:S(2)}) async-start(), calls=%async_computation.4 | async-start | bytes 7864320 | tf_op jit(solution)/shard_map/reduce_scatter | solution.py:72
  71.0 1.5 copy-start.8
  577.4 132.7 %copy-start.1 = (bf16[1024,384]{1,0:T(8,128)(2,1)S(1)}, bf16[1024,384]{1,0:T(8,128)(2,1)}, u32[]{:S(2)}) copy-start(bf16[1024,384]{1,0:T(8,128)(2,1)} %param.14) | copy-start | bytes 2359300
  577.4 218.1 %all-reduce.2.cloned.1.call-start = ((), (), s32[]{:S(2)}) async-start(), calls=%async_computation.5 | async-start | bytes 6291456 | tf_op jit(solution)/shard_map/psum | solution.py:74
  711.7 2.7 copy-start.2
  711.8 2.7 copy-start.6
  711.8 2.9 copy-start.4
  711.8 83.7 %copy-start.12 = (bf16[768,128]{1,0:T(8,128)(2,1)S(1)}, bf16[768,128]{1,0:T(8,128)(2,1)}, u32[]{:S(2)}) copy-start(bf16[768,128]{1,0:T(8,128)(2,1)} %param.19) | copy-start | bytes 589828
  714.9 92.1 %copy-start.7 = (s32[32,32]{1,0:T(8,128)S(1)}, s32[32,32]{1,0:T(8,128)}, u32[]{:S(2)}) copy-start(s32[32,32]{1,0:T(8,128)} %param.21) | copy-start | bytes 12292
  798.5 13.6 %copy-start.5 = (bf16[128,256]{1,0:T(8,128)(2,1)S(1)}, bf16[128,256]{1,0:T(8,128)(2,1)}, u32[]{:S(2)}) copy-start(bf16[128,256]{1,0:T(8,128)(2,1)} %param.23) | copy-start | bytes 196612
  798.5 13.9 %copy-start.3 = (bf16[32,32,256]{2,1,0:T(8,128)(2,1)S(1)}, bf16[32,32,256]{2,1,0:T(8,128)(2,1)}, u32[]{:S(2)}) copy-start(bf16[32,32,256]{2,1,0:T(8,128)(2,1)} %param.20) | copy-start | bytes 1572868
  798.5 8.5 collective-permute-start
  800.9 7.9 collective-permute-start.1
  808.8 19.9 %copy-start.9 = (f32[2,256]{1,0:T(2,128)S(1)}, f32[2,256]{1,0:T(2,128)}, u32[]{:S(2)}) copy-start(f32[2,256]{1,0:T(2,128)} %param.25) | copy-start | bytes 6148
  812.7 8.3 collective-permute-start.2
  814.8 7.4 collective-permute-start.3
  822.3 6.5 collective-permute-start.4
  826.8 7.2 collective-permute-start.5
  834.5 9.9 %copy-start.10 = (bf16[2,256,1024]{2,1,0:T(8,128)(2,1)S(1)}, bf16[2,256,1024]{2,1,0:T(8,128)(2,1)}, u32[]{:S(2)}) copy-start(bf16[2,256,1024]{2,1,0:T(8,128)(2,1)} %param.26) | copy-start | bytes 3145732
  844.4 1.5 copy-start.11
  846.7 8.3 collective-permute-start.6
  848.6 7.5 collective-permute-start.7
  856.2 5.5 collective-permute-start.8
  859.5 7.2 collective-permute-start.9
Sparse Core Ops, SparseCore 0:
  9.8 245.4 all-gather.2
  257.1 301.8 all-gather.4
  577.5 132.5 reduce-scatter.1
  714.6 80.8 all-reduce.1
